TPU v7x, 512 devices: a whole 4x8x8 slice. The times are simulated.
512 devices in a mesh: narrow: 8 (over z_hi, core), wide: 64 (over x, y, z_lo).
Axes of the slice: x: 4, y: 8, z: 8 (z_hi: 4, z_lo: 2; z = z_hi * 2 + z_lo), core: 2. Of those that a mesh axis runs over, the one named last changes fastest.
Arguments:
- images: float32 [65536, 1024], P(('narrow', 'wide')), may hold values from -0.25 to 0.25
- texts: float32 [65536, 1024], P(('narrow', 'wide')), may hold values from -0.25 to 0.25
- lang_ids: int32 [65536], P(('narrow', 'wide')), may hold values from 0 to 108
- lang_table: int32 [109], replicated, may hold values from 1 to 16
- log_scale: float32 [1], replicated, may hold values from 1.5 to 2.5
- bias: float32 [1], replicated, may hold values from -3.5 to -1.5
Outputs:
- grad_images: float32 [65536, 1024], P(('narrow', 'wide'))
- grad_texts: float32 [65536, 1024], P(('narrow', 'wide'))
Inputs may be any that keep to these rules, and one draw needn't show every extreme that they name: lang_ids index lang_table.
All inputs are finite; a program needn't handle non-finite values.
Results may differ from a plain program's by a relative error of at most 0.00011.
Values sent between devices are 32-bit elements; how exact they have to be, the bound alone decides.
A program may use at most 64 MiB of HBM per device.

v0:
```python
import jax
import jax.numpy as jnp
from jax import lax
from jax.sharding import PartitionSpec as P

OFFSETS = 4


def passed_along(value, axis, by):
    size = lax.axis_size(axis)
    return lax.ppermute(value, axis, [(i, (i + by) % size) for i in range(size)])


def normalize(vectors):
    inverse = lax.rsqrt(jnp.sum(vectors * vectors, axis=-1, keepdims=True) + 1e-06)
    return (vectors * inverse, inverse)


def project_back(hat_grad, unit, inverse):
    return inverse * (hat_grad - unit * jnp.sum(unit * hat_grad, axis=-1, keepdims=True))


def product(left, right):
    return jnp.dot(left, right, precision=lax.Precision.HIGHEST, preferred_element_type=jnp.float32)


def on_device(images, texts, lang_ids, lang_table, log_scale, bias):
    block_rows = images.shape[0]
    hop_size = lax.axis_size("wide") // 8
    img_hat, inv_img = normalize(images)
    txt_hat, inv_txt = normalize(texts)
    language_count = lang_table.shape[0]
    one_hot = lang_ids[:, None] == jnp.arange(language_count, dtype=jnp.int32)[None, :]
    table_float = lang_table.astype(jnp.float32)
    pair_weight = jnp.sum(jnp.where(one_hot, table_float[None, :], jnp.float32(0.0)), axis=1) / 8.0
    logit_scale = jnp.exp(log_scale[0])
    logit_bias = bias[0]
    group_rows = lax.all_gather(img_hat, "narrow", axis=0, tiled=True)
    own_index = lax.axis_index("narrow")
    row_ids = jnp.arange(group_rows.shape[0], dtype=jnp.int32)
    col_ids = own_index * block_rows + jnp.arange(block_rows, dtype=jnp.int32)
    positive = row_ids[:, None] == col_ids[None, :]
    text_block, text_weight = (txt_hat, pair_weight)
    image_acc = jnp.zeros(group_rows.shape, jnp.float32)
    text_parts = []
    for offset in range(OFFSETS):
        logits = logit_scale * product(group_rows, text_block.T) + logit_bias
        if offset == 0:
            label_sign = jnp.where(positive, jnp.float32(1.0), jnp.float32(-1.0))
        else:
            label_sign = jnp.float32(-1.0)
        pair_grad = (
            -(logit_scale * text_weight[None, :])
            * label_sign
            * jax.nn.sigmoid(-label_sign * logits)
        )
        text_part = product(pair_grad.T, group_rows)
        image_acc = image_acc + product(pair_grad, text_block)
        text_parts.append(text_part)
        if offset + 1 < OFFSETS:
            text_block, text_weight = passed_along((text_block, text_weight), "wide", hop_size)
    text_grad = text_parts[0]
    for distance in range(1, OFFSETS):
        text_grad = text_grad + passed_along(text_parts[distance], "wide", -distance * hop_size)
    summed = lax.psum_scatter(image_acc, "narrow", scatter_dimension=0, tiled=True)
    grad_images = project_back(summed, img_hat, inv_img)
    grad_texts = project_back(text_grad, txt_hat, inv_txt)
    return (grad_images, grad_texts)


def solution(mesh):
    placed = (
        P(("narrow", "wide"), None),
        P(("narrow", "wide"), None),
        P(("narrow", "wide")),
        P(),
        P(),
        P(),
    )
    return jax.shard_map(
        on_device,
        mesh=mesh,
        in_specs=placed,
        out_specs=(P(("narrow", "wide"), None), P(("narrow", "wide"), None)),
        check_vma=False,
    )
```

profile of v0, /device:TPU:7, one launch (start us, length us, event | category | flops | bytes accessed | tf_op | source)
XLA Modules:
  0.0 197.5 jit_solution(9203485656934361643)
XLA Ops:
  7.2 0.0 all-gather.2.cloned.1.call-start
  7.2 1.2 multiply_reduce_fusion.3
  8.4 1.9 broadcast_multiply_fusion.1
  10.3 0.0 all-gather.2.cloned.1.call-update
  10.3 0.0 reduce-scatter.2.cloned.1.call-start
  10.4 1.2 multiply_reduce_fusion.2
  11.6 1.1 broadcast_multiply_fusion
  12.7 7.5 %collective-permute-start.1 = (f32[128,1024]{1,0:T(8,128)S(1)}, f32[128,1024]{1,0:T(8,128)S(1)}, u32[]{:S(2)}, u32[]{:S(2)}) collective-permute-start(f32[128,1024]{1,0:T(8,128)S(1)} %broadcast_multiply_fusion), channel_id=1, source_target_pairs={{0,8},{1,9},{2,10},{3,11},{4,12},{5,13},{6,14},{7,15},{8,16},{9,17... | collective-permute-start | bytes 1572872 | tf_op jit(solution)/shard_map/ppermute | solution.py:11
  20.9 0.7 convert_element_type.3
  21.5 0.7 select_reduce_fusion
  22.3 1.9 collective-permute-start
  24.9 12.7 %collective-permute-done = f32[128]{0:T(128)S(1)} collective-permute-done((f32[128]{0:T(128)S(1)}, f32[128]{0:T(128)S(1)}, u32[]{:S(2)}, u32[]{:S(2)}) %collective-permute-start) | collective-permute-done | bytes 544 | tf_op jit(solution)/shard_map/ppermute | solution.py:11
  37.5 4.8 %collective-permute-start.2 = (f32[128]{0:T(128)S(1)}, f32[128]{0:T(128)S(1)}, u32[]{:S(2)}, u32[]{:S(2)}) collective-permute-start(f32[128]{0:T(128)S(1)} %collective-permute-done), channel_id=1, source_target_pairs={{0,8},{1,9},{2,10},{3,11},{4,12},{5,13},{6,14},{7,15},{8,16},{9,17... | collective-permute-start | bytes 1544 | tf_op jit(solution)/shard_map/ppermute | solution.py:11
  42.4 0.0 collective-permute-done.1
  42.4 0.0 copy-start.4
  42.4 1.9 collective-permute-start.3
  44.3 2.3 %collective-permute-done.2 = f32[128]{0:T(128)S(1)} collective-permute-done((f32[128]{0:T(128)S(1)}, f32[128]{0:T(128)S(1)}, u32[]{:S(2)}, u32[]{:S(2)}) %collective-permute-start.2) | collective-permute-done | bytes 544 | tf_op jit(solution)/shard_map/ppermute | solution.py:11
  46.7 6.8 %collective-permute-start.4 = (f32[128]{0:T(128)S(1)}, f32[128]{0:T(128)S(1)}, u32[]{:S(2)}, u32[]{:S(2)}) collective-permute-start(f32[128]{0:T(128)S(1)} %collective-permute-done.2), channel_id=1, source_target_pairs={{0,8},{1,9},{2,10},{3,11},{4,12},{5,13},{6,14},{7,15},{8,16},{9,17... | collective-permute-start | bytes 1544 | tf_op jit(solution)/shard_map/ppermute | solution.py:11
  53.5 3.7 %collective-permute-done.4 = f32[128]{0:T(128)S(1)} collective-permute-done((f32[128]{0:T(128)S(1)}, f32[128]{0:T(128)S(1)}, u32[]{:S(2)}, u32[]{:S(2)}) %collective-permute-start.4) | collective-permute-done | bytes 544 | tf_op jit(solution)/shard_map/ppermute | solution.py:11
  57.2 0.0 collective-permute-done.3
  57.2 5.6 %collective-permute-start.5 = (f32[128,1024]{1,0:T(8,128)}, f32[128,1024]{1,0:T(8,128)S(1)}, u32[]{:S(2)}, u32[]{:S(2)}) collective-permute-start(f32[128,1024]{1,0:T(8,128)} %collective-permute-done.3), channel_id=1, source_target_pairs={{0,8},{1,9},{2,10},{3,11},{4,12},{5,13},{6,14},{7,15},{8,16},{9,17... | collective-permute-start | bytes 1572872 | tf_op jit(solution)/shard_map/ppermute | solution.py:11
  62.8 7.3 %all-gather.2.cloned.1.call-done = f32[1024,1024]{1,0:T(8,128)} async-done(((f32[128,1024]{1,0:T(8,128)}), f32[1024,1024]{1,0:T(8,128)}) %all-gather.2.cloned.1.call-update) | async-done | bytes 4194320 | tf_op jit(solution)/shard_map/all_gather | solution.py:38
  70.1 0.0 copy-start
  70.1 5.9 %fusion.13 = f32[1024,128]{1,0:T(8,128)S(1)} fusion(f32[1024,1024]{1,0:T(8,128)} %all-gather.2.cloned.1.call-done, f32[128,1024]{1,0:T(8,128)} %collective-permute-done.3, f32[]{:T(128)} %bitcast.22, f32[]{:T(128)} %bitcast), kind=kOutput, calls=%fused_computation.19 | convolution fusion | flops 1611268096 | bytes 5242888 | tf_op jit(solution)/shard_map/dot_general | solution.py:24
  76.1 0.0 copy-done
  76.1 3.4 %fusion.23 = f32[1024,128]{1,0:T(8,128)S(1)} fusion(f32[1024,1024]{1,0:T(8,128)S(1)} %copy-done, f32[128,1024]{1,0:T(8,128)S(1)} %broadcast_multiply_fusion, f32[]{:T(128)} %bitcast.20, f32[]{:T(128)} %bitcast, s32[128]{0:T(128)S(1)} %iota_add_fusion, f32[128]{0:T(128)S(1)} %get-tuple-element.2), kind=kOutput, calls=%fused_computation.29 | convolution fusion | flops 1612054528 | bytes 5243912 | tf_op jit(solution)/shard_map/dot_general | solution.py:24
  79.5 3.4 %fusion.41 = f32[1024,1024]{1,0:T(8,128)S(1)} fusion(f32[1024,128]{1,0:T(8,128)S(1)} %fusion.23, f32[128,1024]{1,0:T(8,128)S(1)} %broadcast_multiply_fusion), kind=kOutput, calls=%fused_computation.68 | convolution fusion | flops 1610612736 | bytes 5242880 | tf_op jit(solution)/shard_map/dot_general | solution.py:24
  82.9 0.0 copy-done.4
  83.0 3.4 %fusion.8 = f32[1024,128]{1,0:T(8,128)S(1)} fusion(f32[1024,1024]{1,0:T(8,128)S(1)} %copy-done, f32[128,1024]{1,0:T(8,128)S(1)} %collective-permute-done.1, f32[]{:T(128)} %bitcast.23, f32[]{:T(128)} %bitcast), kind=kOutput, calls=%fused_computation.14 | convolution fusion | flops 1611268096 | bytes 5242888 | tf_op jit(solution)/shard_map/dot_general | solution.py:24
  86.4 0.0 collective-permute-done.5
  86.4 0.0 copy-start.5
  86.4 3.6 %fusion.18 = f32[1024,128]{1,0:T(8,128)S(1)} fusion(f32[1024,1024]{1,0:T(8,128)S(1)} %copy-done, f32[128,1024]{1,0:T(8,128)S(1)} %collective-permute-done.5, f32[]{:T(128)} %bitcast.21, f32[]{:T(128)} %bitcast), kind=kOutput, calls=%fused_computation.24 | convolution fusion | flops 1611268096 | bytes 5242888 | tf_op jit(solution)/shard_map/dot_general | solution.py:24
  90.0 4.5 %fusion.29 = f32[1024,1024]{1,0:T(8,128)S(1)} fusion(f32[128,1024]{1,0:T(8,128)} %collective-permute-done.3, f32[1024,128]{1,0:T(8,128)S(1)} %fusion.13, f32[128]{0:T(128)S(1)} %negate_multiply_fusion.1), kind=kOutput, calls=%fused_computation.44 | convolution fusion | flops 1610743808 | bytes 5243392 | tf_op jit(solution)/shard_map/dot_general | solution.py:24
  94.5 0.0 copy-done.5
  94.5 3.4 %fusion.33 = f32[1024,1024]{1,0:T(8,128)S(1)} fusion(f32[128,1024]{1,0:T(8,128)S(1)} %copy-done.5, f32[1024,128]{1,0:T(8,128)S(1)} %fusion.8, f32[128]{0:T(128)S(1)} %negate_multiply_fusion.2), kind=kOutput, calls=%fused_computation.48 | convolution fusion | flops 1610743808 | bytes 5243392 | tf_op jit(solution)/shard_map/dot_general | solution.py:24
  98.0 5.6 %add_add_fusion = f32[1024,1024]{1,0:T(8,128)} fusion(f32[1024,1024]{1,0:T(8,128)S(1)} %fusion.29, f32[1024,1024]{1,0:T(8,128)S(1)} %fusion.41, f32[1024,1024]{1,0:T(8,128)S(1)} %fusion.33, f32[128,1024]{1,0:T(8,128)S(1)} %collective-permute-done.5, f32[1024,128]{1,0:T(8,128)S(1)} %fusion.18, f32[128]{0:T(128)S(1)} %negate_multiply_fusion), kind=kOutput, calls=%fused_computation | convolution fusion | flops 1613889536 | bytes 17826304 | tf_op jit(solution)/shard_map/dot_general | solution.py:24
  103.6 0.0 reduce-scatter.2.cloned.1.call-update
  103.6 0.0 copy-start.1
  103.6 4.7 %fusion.24 = f32[128,1024]{1,0:T(8,128)S(1)} fusion(f32[1024,1024]{1,0:T(8,128)} %all-gather.2.cloned.1.call-done, f32[1024,128]{1,0:T(8,128)S(1)} %fusion.18, f32[128]{0:T(128)S(1)} %negate_multiply_fusion), kind=kOutput, calls=%fused_computation.39 | convolution fusion | flops 1610743808 | bytes 5243392 | tf_op jit(solution)/shard_map/dot_general | solution.py:24
  108.4 9.0 %collective-permute-start.8 = (f32[128,1024]{1,0:T(8,128)S(1)}, f32[128,1024]{1,0:T(8,128)S(1)}, u32[]{:S(2)}, u32[]{:S(2)}) collective-permute-start(f32[128,1024]{1,0:T(8,128)S(1)} %fusion.24), channel_id=1, source_target_pairs={{0,40},{1,41},{2,42},{3,43},{4,44},{5,45},{6,46},{7,47},{8,48},{9,... | collective-permute-start | bytes 1572872 | tf_op jit(solution)/shard_map/ppermute | solution.py:11
  117.4 0.0 copy-done.1
  117.4 2.4 %fusion.27 = f32[128,1024]{1,0:T(8,128)S(1)} fusion(f32[1024,1024]{1,0:T(8,128)S(1)} %copy-done.1, f32[1024,128]{1,0:T(8,128)S(1)} %fusion.13, f32[128]{0:T(128)S(1)} %negate_multiply_fusion.1), kind=kOutput, calls=%fused_computation.42 | convolution fusion | flops 1610743808 | bytes 5243392 | tf_op jit(solution)/shard_map/dot_general | solution.py:24
  119.8 1.9 collective-permute-start.7
  121.7 2.4 %fusion.31 = f32[128,1024]{1,0:T(8,128)S(1)} fusion(f32[1024,1024]{1,0:T(8,128)S(1)} %copy-done.1, f32[1024,128]{1,0:T(8,128)S(1)} %fusion.8, f32[128]{0:T(128)S(1)} %negate_multiply_fusion.2), kind=kOutput, calls=%fused_computation.46 | convolution fusion | flops 1610743808 | bytes 5243392 | tf_op jit(solution)/shard_map/dot_general | solution.py:24
  124.2 0.0 copy-start.3
  124.2 0.0 copy-start.2
  124.2 16.3 %collective-permute-start.6 = (f32[128,1024]{1,0:T(8,128)S(1)}, f32[128,1024]{1,0:T(8,128)S(1)}, u32[]{:S(2)}, u32[]{:S(2)}) collective-permute-start(f32[128,1024]{1,0:T(8,128)S(1)} %fusion.31), channel_id=1, source_target_pairs={{0,56},{1,57},{2,58},{3,59},{4,60},{5,61},{6,62},{7,63},{8,0},{9,1... | collective-permute-start | bytes 1572872 | tf_op jit(solution)/shard_map/ppermute | solution.py:11
  140.5 0.0 collective-permute-done.8
  140.5 0.0 collective-permute-done.7
  140.5 26.2 %collective-permute-done.6 = f32[128,1024]{1,0:T(8,128)S(1)} collective-permute-done((f32[128,1024]{1,0:T(8,128)S(1)}, f32[128,1024]{1,0:T(8,128)S(1)}, u32[]{:S(2)}, u32[]{:S(2)}) %collective-permute-start.6) | collective-permute-done | bytes 524320 | tf_op jit(solution)/shard_map/ppermute | solution.py:11
  166.7 2.6 %multiply_reduce_fusion = (f32[128]{0:T(128)S(1)}, f32[128,1024]{1,0:T(8,128)S(1)}) fusion(f32[128,1024]{1,0:T(8,128)S(1)} %broadcast_multiply_fusion, f32[128,1024]{1,0:T(8,128)S(1)} %collective-permute-done.8, f32[128,1024]{1,0:T(8,128)S(1)} %collective-permute-done.7, f32[128,1024]{1,0:T(8,128)S(1)} %collective-permute-done.6, ...), kind=kOutput, calls=%fused_computation.33 | convolution fusion | flops 1611267968 | bytes 7340544 | tf_op jit(solution)/shard_map/dot_general | solution.py:24
  169.3 0.0 copy-done.3
  169.3 1.0 subtract_multiply_fusion
  170.2 17.0 %reduce-scatter.2.cloned.1.call-done = f32[128,1024]{1,0:T(8,128)} async-done(((f32[1024,1024]{1,0:T(8,128)}), f32[128,1024]{1,0:T(8,128)}) %reduce-scatter.2.cloned.1.call-update) | async-done | bytes 524304 | tf_op jit(solution)/shard_map/reduce_scatter | solution.py:65
  187.2 0.0 copy-done.2
  187.2 1.2 multiply_reduce_fusion.1
  188.5 2.0 %subtract_multiply_fusion.1 = f32[128,1024]{1,0:T(8,128)} fusion(f32[128,1024]{1,0:T(8,128)} %reduce-scatter.2.cloned.1.call-done, f32[128]{0:T(128)S(1)} %multiply_reduce_fusion.1, f32[128]{0:T(128)S(1)} %add_rsqrt_fusion.1, f32[128,1024]{1,0:T(8,128)S(1)} %copy-done.2), kind=kLoop, calls=%fused_computation.34 | loop fusion | flops 524288 | bytes 1573888 | tf_op jit(solution)/shard_map/mul | solution.py:20
  (7 shorter events, 0.0 us)
Async XLA Ops:
  7.2 63.0 %all-gather.2.cloned.1.call-start = ((), (), s32[]{:S(2)}) async-start(), calls=%async_computation.1 | async-start | bytes 4718592 | tf_op jit(solution)/shard_map/all_gather | solution.py:38
  10.3 176.9 %reduce-scatter.2.cloned.1.call-start = ((), (), s32[]{:S(2)}) async-start(), calls=%async_computation.2 | async-start | bytes 4718592 | tf_op jit(solution)/shard_map/reduce_scatter | solution.py:65
  12.7 29.6 %collective-permute-start.1 = (f32[128,1024]{1,0:T(8,128)S(1)}, f32[128,1024]{1,0:T(8,128)S(1)}, u32[]{:S(2)}, u32[]{:S(2)}) collective-permute-start(f32[128,1024]{1,0:T(8,128)S(1)} %broadcast_multiply_fusion), channel_id=1, source_target_pairs={{0,8},{1,9},{2,10},{3,11},{4,12},{5,13},{6,14},{7,15},{8,16},{9,17... | collective-permute-start | bytes 1572872 | tf_op jit(solution)/shard_map/ppermute | solution.py:11
  22.3 15.2 %collective-permute-start = (f32[128]{0:T(128)S(1)}, f32[128]{0:T(128)S(1)}, u32[]{:S(2)}, u32[]{:S(2)}) collective-permute-start(f32[128]{0:T(128)S(1)} %get-tuple-element.3), channel_id=1, source_target_pairs={{0,8},{1,9},{2,10},{3,11},{4,12},{5,13},{6,14},{7,15},{8,16},{9,17... | collective-permute-start | bytes 1544 | tf_op jit(solution)/shard_map/ppermute | solution.py:11
  37.5 9.1 %collective-permute-start.2 = (f32[128]{0:T(128)S(1)}, f32[128]{0:T(128)S(1)}, u32[]{:S(2)}, u32[]{:S(2)}) collective-permute-start(f32[128]{0:T(128)S(1)} %collective-permute-done), channel_id=1, source_target_pairs={{0,8},{1,9},{2,10},{3,11},{4,12},{5,13},{6,14},{7,15},{8,16},{9,17... | collective-permute-start | bytes 1544 | tf_op jit(solution)/shard_map/ppermute | solution.py:11
  42.4 40.6 %copy-start.4 = (f32[128,1024]{1,0:T(8,128)}, f32[128,1024]{1,0:T(8,128)S(1)}, u32[]{:S(2)}) copy-start(f32[128,1024]{1,0:T(8,128)S(1)} %collective-permute-done.1) | copy-start | bytes 1572868
  42.4 14.9 %collective-permute-start.3 = (f32[128,1024]{1,0:T(8,128)S(1)}, f32[128,1024]{1,0:T(8,128)}, u32[]{:S(2)}, u32[]{:S(2)}) collective-permute-start(f32[128,1024]{1,0:T(8,128)S(1)} %collective-permute-done.1), channel_id=1, source_target_pairs={{0,8},{1,9},{2,10},{3,11},{4,12},{5,13},{6,14},{7,15},{8,16},{9,17... | collective-permute-start | bytes 1572872 | tf_op jit(solution)/shard_map/ppermute | solution.py:11
  46.7 10.6 %collective-permute-start.4 = (f32[128]{0:T(128)S(1)}, f32[128]{0:T(128)S(1)}, u32[]{:S(2)}, u32[]{:S(2)}) collective-permute-start(f32[128]{0:T(128)S(1)} %collective-permute-done.2), channel_id=1, source_target_pairs={{0,8},{1,9},{2,10},{3,11},{4,12},{5,13},{6,14},{7,15},{8,16},{9,17... | collective-permute-start | bytes 1544 | tf_op jit(solution)/shard_map/ppermute | solution.py:11
  57.2 29.1 %collective-permute-start.5 = (f32[128,1024]{1,0:T(8,128)}, f32[128,1024]{1,0:T(8,128)S(1)}, u32[]{:S(2)}, u32[]{:S(2)}) collective-permute-start(f32[128,1024]{1,0:T(8,128)} %collective-permute-done.3), channel_id=1, source_target_pairs={{0,8},{1,9},{2,10},{3,11},{4,12},{5,13},{6,14},{7,15},{8,16},{9,17... | collective-permute-start | bytes 1572872 | tf_op jit(solution)/shard_map/ppermute | solution.py:11
  70.1 5.9 %copy-start = (f32[1024,1024]{1,0:T(8,128)S(1)}, f32[1024,1024]{1,0:T(8,128)}, u32[]{:S(2)}) copy-start(f32[1024,1024]{1,0:T(8,128)} %all-gather.2.cloned.1.call-done) | copy-start | bytes 12582916
  86.4 8.1 %copy-start.5 = (f32[128,1024]{1,0:T(8,128)S(1)}, f32[128,1024]{1,0:T(8,128)}, u32[]{:S(2)}) copy-start(f32[128,1024]{1,0:T(8,128)} %copy-done.4) | copy-start | bytes 1572868
  103.6 13.8 %copy-start.1 = (f32[1024,1024]{1,0:T(8,128)S(1)}, f32[1024,1024]{1,0:T(8,128)}, u32[]{:S(2)}) copy-start(f32[1024,1024]{1,0:T(8,128)} %all-gather.2.cloned.1.call-done) | copy-start | bytes 12582916
  108.4 32.1 %collective-permute-start.8 = (f32[128,1024]{1,0:T(8,128)S(1)}, f32[128,1024]{1,0:T(8,128)S(1)}, u32[]{:S(2)}, u32[]{:S(2)}) collective-permute-start(f32[128,1024]{1,0:T(8,128)S(1)} %fusion.24), channel_id=1, source_target_pairs={{0,40},{1,41},{2,42},{3,43},{4,44},{5,45},{6,46},{7,47},{8,48},{9,... | collective-permute-start | bytes 1572872 | tf_op jit(solution)/shard_map/ppermute | solution.py:11
  119.8 20.7 %collective-permute-start.7 = (f32[128,1024]{1,0:T(8,128)S(1)}, f32[128,1024]{1,0:T(8,128)S(1)}, u32[]{:S(2)}, u32[]{:S(2)}) collective-permute-start(f32[128,1024]{1,0:T(8,128)S(1)} %fusion.27), channel_id=1, source_target_pairs={{0,48},{1,49},{2,50},{3,51},{4,52},{5,53},{6,54},{7,55},{8,56},{9,... | collective-permute-start | bytes 1572872 | tf_op jit(solution)/shard_map/ppermute | solution.py:11
  124.2 45.1 %copy-start.3 = (f32[128,1024]{1,0:T(8,128)S(1)}, f32[128,1024]{1,0:T(8,128)}, u32[]{:S(2)}) copy-start(f32[128,1024]{1,0:T(8,128)} %param.7) | copy-start | bytes 1572868
  124.2 63.1 %copy-start.2 = (f32[128,1024]{1,0:T(8,128)S(1)}, f32[128,1024]{1,0:T(8,128)}, u32[]{:S(2)}) copy-start(f32[128,1024]{1,0:T(8,128)} %param.6) | copy-start | bytes 1572868
  124.2 42.5 %collective-permute-start.6 = (f32[128,1024]{1,0:T(8,128)S(1)}, f32[128,1024]{1,0:T(8,128)S(1)}, u32[]{:S(2)}, u32[]{:S(2)}) collective-permute-start(f32[128,1024]{1,0:T(8,128)S(1)} %fusion.31), channel_id=1, source_target_pairs={{0,56},{1,57},{2,58},{3,59},{4,60},{5,61},{6,62},{7,63},{8,0},{9,1... | collective-permute-start | bytes 1572872 | tf_op jit(solution)/shard_map/ppermute | solution.py:11
Sparse Core Ops, SparseCore 0:
  10.7 59.3 all-gather.1
  103.7 83.4 reduce-scatter.1
where the time goes:
time: 201 us; the launch traced here: 198 us
  waiting for transfers between devices  69.2 us (34%)
  starting transfers between devices  55.8 us (28%)
  matrix products  45.5 us (23%)
  between operations  15.9 us (8%)
  other arithmetic  11.1 us (6%)
    ppermute x9, starting transfers between devices, passed_along(): lax.ppermute(value, axis, [(i, (i + by) % size) for i in range(size)])  55.8 us
    dot_general x12, matrix products, product(): jnp.dot(left, right, precision=lax.Precision.HIGHEST, preferred_element_t...  45.5 us
    ppermute x9, waiting for transfers between devices, passed_along(): lax.ppermute(value, axis, [(i, (i + by) % size) for i in range(size)])  44.9 us
    reduce_scatter x1, waiting for transfers between devices, on_device(): lax.psum_scatter(image_acc, 'narrow', scatter_dimension=0, tiled=True)  17 us
    all_gather x1, waiting for transfers between devices, on_device(): group_rows = lax.all_gather(img_hat, 'narrow', axis=0, tiled=True)  7.27 us
  transfers between devices with their start and end apart: 11, of which 6 were waited for; matrix products, arithmetic and copies ran while one was open for 17% of the time, Pallas kernels for 0%

commit v1 on v0

v1 whole, which is shorter than its diff:
```python
import jax
import jax.numpy as jnp
from jax import lax
from jax.experimental import pallas as pl
from jax.experimental.pallas import tpu as pltpu
from jax.sharding import PartitionSpec as P

MESH = pl.DeviceIdType.MESH
OFFSETS = 4
ROWS = 128
HALF = 64
DIM = 1024
PAIR = 2 * ROWS
NARROW = 8
WIDE = 64
PREV, NEXT, OWN, OPP = 0, 1, 2, 3
QUARTER = 32
COPIES = tuple(
    ["ia", "ib", "ja", "jb", "fa", "fb", "t1a", "t1b", "t2", "t3a", "t3b", "u2"]
    + ["w1", "w2", "w3", "ha", "hb", "sa", "sb", "dn0", "dn1", "dp0", "dp1"]
    + [f"{name}{i}" for name in ("u3", "v1", "sw", "s", "q") for i in range(4)]
)


def split(value):
    high = value.astype(jnp.bfloat16)
    low = (value - high.astype(jnp.float32)).astype(jnp.bfloat16)
    return high, low


def dot3(left, right, left_dim, right_dim):
    dims = (((left_dim,), (right_dim,)), ((), ()))

    def one(a, b):
        return lax.dot_general(a, b, dims, preferred_element_type=jnp.float32)

    return one(left[0], right[0]) + (one(left[1], right[0]) + one(left[0], right[1]))


def kernel(
    img_hbm, txt_hbm, ids_hbm, table_hbm, scale_hbm, bias_hbm, img_sum, txt_sum,
    raw, ids_ref, table_ref, scale_ref, bias_ref, load_sem, img, txt, wts, img_h, img_l, txt_h, txt_l, g_h, g_l, img_part, txt_part,
    half_a, half_b, from_prev, from_next, sib_part, got3, got1, got2, send_sem, recv_sem,
):
    n = lax.axis_index("narrow")
    w = lax.axis_index("wide")
    nxt = (lax.rem(n + 2, NARROW), w)
    prv = (lax.rem(n + NARROW - 2, NARROW), w)
    sib = (n + 1 - 2 * lax.rem(n, 2), w)
    hop = WIDE // 8
    step1, back1 = (n, lax.rem(w + hop, WIDE)), (n, lax.rem(w + WIDE - hop, WIDE))
    step2, back2 = (n, lax.rem(w + 2 * hop, WIDE)), (n, lax.rem(w + WIDE - 2 * hop, WIDE))

    barrier = pltpu.get_barrier_semaphore()
    partners = (nxt, prv, sib, step1, back1, step2, back2)
    for partner in partners:
        pl.semaphore_signal(barrier, inc=1, device_id=partner, device_id_type=MESH)

    A, B = pl.ds(0, HALF), pl.ds(HALF, HALF)
    part = [pl.ds(i * QUARTER, QUARTER) for i in range(4)]
    plan = {
        "ia": (img.at[OWN, A], img.at[PREV, A], nxt),
        "ib": (img.at[OWN, B], img.at[PREV, B], nxt),
        "ja": (img.at[OWN, A], img.at[NEXT, A], prv),
        "jb": (img.at[OWN, B], img.at[NEXT, B], prv),
        "fa": (img.at[PREV, A], img.at[OPP, A], nxt),
        "fb": (img.at[NEXT, B], img.at[OPP, B], prv),
        "ha": (img_part.at[OPP, A], half_a, nxt),
        "hb": (img_part.at[OPP, B], half_b, prv),
        "sa": (img_part.at[NEXT, A], from_prev.at[A], nxt),
        "sb": (img_part.at[PREV, B], from_next.at[B], prv),
        "t1a": (txt.at[0, 0, A], txt.at[1, 0, A], step1),
        "t1b": (txt.at[0, 0, B], txt.at[1, 0, B], step1),
        "t3a": (txt.at[1, 0, A], txt.at[3, 0, A], step2),
        "t3b": (txt.at[1, 0, B], txt.at[3, 0, B], step2),
        "t2": (txt.at[0, 0], txt.at[2, 0], step2),
        "u2": (txt_part.at[2, 0], got2, back2),
        "w1": (wts.at[0, 0], wts.at[1, 0], step1),
        "w2": (wts.at[0, 0], wts.at[2, 0], step2),
        "w3": (wts.at[1, 0], wts.at[3, 0], step2),
    }
    for i in range(4):
        plan[f"u3{i}"] = (txt_part.at[3, 0, part[i]], got3.at[part[i]], back2)
        plan[f"v1{i}"] = (txt_part.at[1, 0, part[i]], got1.at[part[i]], back1)
        plan[f"sw{i}"] = (wts.at[i, 0], wts.at[i, 1], sib)
        plan[f"s{i}"] = (txt.at[i, 0], txt.at[i, 1], sib)
        plan[f"q{i}"] = (txt_part.at[i, 1], sib_part.at[i], sib)
    for i in range(2):
        low, high = part[i], part[2 + i]
        plan[f"dn{i}"] = (img_part.at[NEXT, high], from_prev.at[high], nxt)
        plan[f"dp{i}"] = (img_part.at[PREV, low], from_next.at[low], prv)

    def copy(name):
        src, dst, device = plan[name]
        i = COPIES.index(name)
        return pltpu.make_async_remote_copy(
            src_ref=src, dst_ref=dst, send_sem=send_sem.at[i], recv_sem=recv_sem.at[i],
            device_id=device, device_id_type=MESH,
        )

    def start(*names):
        for name in names:
            copy(name).start()

    done = set()

    def sent(*names):
        for name in names:
            copy(name).wait_send()
            done.add(name)

    def arrived(*names):
        for name in names:
            copy(name).wait_recv()

    loads = [
        pltpu.make_async_copy(src, dst, load_sem.at[i])
        for i, (src, dst) in enumerate(
            [(img_hbm, raw.at[0]), (txt_hbm, raw.at[1]), (ids_hbm, ids_ref),
             (table_hbm, table_ref), (scale_hbm, scale_ref), (bias_hbm, bias_ref)]
        )
    ]
    for load in loads:
        load.start()

    def unit_rows(which):
        rows = raw[which]
        return rows * lax.rsqrt(jnp.sum(rows * rows, axis=-1, keepdims=True) + 1e-06)

    loads[0].wait()
    img[OWN] = unit_rows(0)
    pl.semaphore_wait(barrier, len(partners))
    start("ia", "jb", "ib", "ja")
    loads[1].wait()
    txt[0, 0] = unit_rows(1)
    start("t1a", "t1b", "t2", "s0")
    for load in loads[2:]:
        load.wait()
    ids = jnp.broadcast_to(ids_ref[...], (8, ROWS))
    weight = jnp.zeros((8, ROWS), jnp.int32)
    for language in range(table_ref.shape[0]):
        weight = jnp.where(ids == language, table_ref[language], weight)
    wts[0, 0] = weight.astype(jnp.float32) / 8.0
    start("w1", "w2", "sw0")

    logit_scale = jnp.exp(jnp.full((1, ROWS), scale_ref[0], jnp.float32))[:, :1]
    logit_bias = bias_ref[0]

    def split_image(slot):
        rows = pl.ds(slot * ROWS, ROWS)
        img_h[rows, :], img_l[rows, :] = split(img[slot])

    def split_text(k, side):
        rows = pl.ds(k * PAIR + side * ROWS, ROWS)
        txt_h[rows, :], txt_l[rows, :] = split(txt[k, side])

    def pair_grads(first, count, k):
        rows, cols = pl.ds(first * ROWS, count * ROWS), pl.ds(k * PAIR, PAIR)
        dots = dot3((img_h[rows, :], img_l[rows, :]), (txt_h[cols, :], txt_l[cols, :]), 1, 1)
        logits = logit_scale * dots + logit_bias
        pair_w = jnp.concatenate([wts[k, 0, 0:1, :], wts[k, 1, 0:1, :]], axis=1)
        factor = jnp.broadcast_to(logit_scale * pair_w, logits.shape)
        if k == 0 and first <= OWN < first + count:
            row = lax.broadcasted_iota(jnp.int32, logits.shape, 0) - (OWN - first) * ROWS
            positive = row == lax.broadcasted_iota(jnp.int32, logits.shape, 1)
            logits = jnp.where(positive, -logits, logits)
            factor = jnp.where(positive, -factor, factor)
        grads = factor / (1.0 + jnp.exp(-logits))
        g_h[rows, cols], g_l[rows, cols] = split(grads)

    def image_grads(first, count):
        rows = pl.ds(first * ROWS, count * ROWS)
        for tile in range(DIM // PAIR):
            cols = pl.ds(tile * PAIR, PAIR)
            part = dot3((g_h[rows, :], g_l[rows, :]), (txt_h[:, cols], txt_l[:, cols]), 1, 0)
            for slot in range(count):
                img_part[first + slot, :, cols] = part[slot * ROWS:(slot + 1) * ROWS]

    def text_grads(k):
        rows = pl.ds(k * PAIR, PAIR)
        for tile in range(DIM // PAIR):
            cols = pl.ds(tile * PAIR, PAIR)
            part = dot3((g_h[:, rows], g_l[:, rows]), (img_h[:, cols], img_l[:, cols]), 0, 0)
            txt_part[k, 0, :, cols] = part[:ROWS]
            txt_part[k, 1, :, cols] = part[ROWS:]

    split_image(OWN)
    split_text(0, 0)
    arrived("s0", "sw0")
    split_text(0, 1)

    arrived("ia")
    start("fa")
    arrived("jb")
    start("fb")
    arrived("t1a")
    start("t3a")
    arrived("t2")
    start("s2")
    arrived("w1", "w2")
    start("w3", "sw1", "sw2")
    arrived("t1b")
    start("t3b", "s1")
    arrived("ib")
    split_image(PREV)
    arrived("ja")
    split_image(NEXT)
    split_text(1, 0)
    split_text(2, 0)
    pair_grads(PREV, 3, 0)
    arrived("s2", "sw2")
    split_text(2, 1)
    pair_grads(PREV, 3, 2)
    arrived("s1", "sw1")
    split_text(1, 1)
    pair_grads(PREV, 3, 1)
    arrived("w3")
    start("sw3")
    arrived("t3a", "t3b")
    start("s3")
    split_text(3, 0)
    arrived("s3", "sw3")
    split_text(3, 1)
    pair_grads(PREV, 3, 3)
    image_grads(PREV, 2)
    start("dn0", "dp0")

    arrived("fa", "fb")
    split_image(OPP)
    pair_grads(OPP, 1, 3)
    text_grads(3)
    start("q3")
    pair_grads(OPP, 1, 1)
    pair_grads(OPP, 1, 0)
    arrived("q3")
    txt_part[3, 0] += sib_part[3]
    start("u30")
    pair_grads(OPP, 1, 2)
    image_grads(OPP, 1)
    start("ha", "hb")
    text_grads(1)
    start("q1")
    sent("u30")
    start("u31")
    text_grads(2)
    start("q2")
    arrived("q1")
    txt_part[1, 0] += sib_part[1]
    for i in range(4):
        arrived(f"u3{i}")
        txt_part[1, 0, part[i]] += got3[part[i]]
        start(f"v1{i}")
        if i < 2:
            sent(f"u3{i + 1}")
            start(f"u3{i + 2}")
        if i == 0:
            text_grads(0)
            start("q0")
        if i == 1:
            image_grads(OWN, 1)
    arrived("q2")
    txt_part[2, 0] += sib_part[2]
    sent("u33")
    start("u2")
    sent("ha", "hb")
    start("dn1", "dp1")
    arrived("ha")
    img_part[NEXT, A] += half_a[...]
    start("sa")
    arrived("hb")
    img_part[PREV, B] += half_b[...]
    start("sb")
    arrived("q0")
    txt_part[0, 0] += sib_part[0]

    arrived("dn0", "dn1", "dp0", "dp1", "sa", "sb")
    img_sum[...] = img_part[OWN] + from_prev[...] + from_next[...]
    arrived("u2", "v10", "v11", "v12", "v13")
    txt_sum[...] = txt_part[0, 0] + got1[...] + got2[...]
    for name in COPIES:
        if name not in done:
            copy(name).wait_send()


def project_back(img_ref, txt_ref, img_sum, txt_sum, gimg_ref, gtxt_ref):
    for rows, total, out in ((img_ref, img_sum, gimg_ref), (txt_ref, txt_sum, gtxt_ref)):
        vectors = rows[...]
        inverse = lax.rsqrt(jnp.sum(vectors * vectors, axis=-1, keepdims=True) + 1e-06)
        unit = vectors * inverse
        hat_grad = total[...]
        along = jnp.sum(unit * hat_grad, axis=-1, keepdims=True)
        out[...] = inverse * (hat_grad - unit * along)


def on_device(images, texts, lang_ids, lang_table, log_scale, bias):
    vmem = pl.BlockSpec(memory_space=pltpu.VMEM)
    anywhere = pl.BlockSpec(memory_space=pl.ANY)
    f32, bf16 = jnp.float32, jnp.bfloat16
    block = (ROWS, DIM)
    half = (HALF, DIM)
    out = jax.ShapeDtypeStruct(block, f32)
    img_sum, txt_sum = pl.pallas_call(
        kernel,
        out_shape=(out, out),
        in_specs=[anywhere] * 6,
        out_specs=(vmem, vmem),
        scratch_shapes=[
            pltpu.VMEM((2,) + block, f32),
            pltpu.VMEM((1, ROWS), jnp.int32),
            pltpu.SMEM(lang_table.shape, jnp.int32),
            pltpu.SMEM((1,), f32),
            pltpu.SMEM((1,), f32),
            pltpu.SemaphoreType.DMA((6,)),
            pltpu.VMEM((4,) + block, f32),
            pltpu.VMEM((4, 2) + block, f32),
            pltpu.VMEM((4, 2, 8, ROWS), f32),
            pltpu.VMEM((4 * ROWS, DIM), bf16),
            pltpu.VMEM((4 * ROWS, DIM), bf16),
            pltpu.VMEM((4 * PAIR, DIM), bf16),
            pltpu.VMEM((4 * PAIR, DIM), bf16),
            pltpu.VMEM((4 * ROWS, 4 * PAIR), bf16),
            pltpu.VMEM((4 * ROWS, 4 * PAIR), bf16),
            pltpu.VMEM((4,) + block, f32),
            pltpu.VMEM((4, 2) + block, f32),
            pltpu.VMEM(half, f32),
            pltpu.VMEM(half, f32),
            pltpu.VMEM(block, f32),
            pltpu.VMEM(block, f32),
            pltpu.VMEM((4,) + block, f32),
            pltpu.VMEM(block, f32),
            pltpu.VMEM(block, f32),
            pltpu.VMEM(block, f32),
            pltpu.SemaphoreType.DMA((len(COPIES),)),
            pltpu.SemaphoreType.DMA((len(COPIES),)),
        ],
        compiler_params=pltpu.CompilerParams(
            collective_id=0, has_side_effects=True, vmem_limit_bytes=56 * 2**20
        ),
        cost_estimate=pl.CostEstimate(
            flops=9 * 2 * 512 * 1024 * 1024, bytes_accessed=4 * 2**19, transcendentals=2**19
        ),
    )(images, texts, lang_ids.reshape(1, ROWS), lang_table, log_scale, bias)
    return pl.pallas_call(
        project_back,
        out_shape=(out, out),
        in_specs=[vmem] * 4,
        out_specs=(vmem, vmem),
        cost_estimate=pl.CostEstimate(flops=2**20, bytes_accessed=6 * 2**19, transcendentals=256),
    )(images, texts, img_sum, txt_sum)


def solution(mesh):
    placed = (
        P(("narrow", "wide"), None),
        P(("narrow", "wide"), None),
        P(("narrow", "wide")),
        P(),
        P(),
        P(),
    )
    return jax.shard_map(
        on_device,
        mesh=mesh,
        in_specs=placed,
        out_specs=(P(("narrow", "wide"), None), P(("narrow", "wide"), None)),
        check_vma=False,
    )
```

time: 201 us -> 104 us (0.52)
  the two profiles are of different devices: /device:TPU:7 before, /device:TPU:104 now
where the time goes in v1:
time: 104 us; the launch traced here: 103 us
  Pallas kernels  101 us (97%)
  between operations  1.93 us (2%)
    pallas_call x1, Pallas kernels, on_device(): pl.pallas_call(kernel, out_shape=(out, out), in_specs=[anywhere] * 6, out...  98.7 us
    pallas_call x1, Pallas kernels, on_device(): pl.pallas_call(project_back, out_shape=(out, out), in_specs=[vmem] * 4, o...  2.75 us

profile of v1, /device:TPU:104, one launch (start us, length us, event | category | flops | bytes accessed | tf_op | source)
XLA Modules:
  0.0 103.4 jit_solution(6181815572140802451)
XLA Ops:
  1.9 98.7 %shard_map.77 = (f32[128,1024]{1,0:T(8,128)}, f32[128,1024]{1,0:T(8,128)}) custom-call(f32[128,1024]{1,0:T(8,128)} %img_ref.1, f32[128,1024]{1,0:T(8,128)} %txt_ref.1, s32[1,128]{1,0:T(1,128)} %bitcast.1, s32[109]{0:T(128)} %table_hbm.1, f32[1]{0:T(128)S(6)} %copy.8.scale_hbm, f32[1]{0:T(128)S(6)} %copy.9.bias_hbm), custom_call_target="tpu_custom_call" | custom-call | flops 9663676416 | bytes 2097152 | tf_op jit(solution)/shard_map/pallas_call | solution.py:302
  100.7 2.7 %shard_map.78 = (f32[128,1024]{1,0:T(8,128)}, f32[128,1024]{1,0:T(8,128)}) custom-call(f32[128,1024]{1,0:T(8,128)} %img_ref.1, f32[128,1024]{1,0:T(8,128)} %txt_ref.1, f32[128,1024]{1,0:T(8,128)} %get-tuple-element.4.img_sum, f32[128,1024]{1,0:T(8,128)} %get-tuple-element.5.txt_sum), custom_call_target="tpu_custom_call" | custom-call | flops 1048576 | bytes 3145728 | tf_op jit(solution)/shard_map/pallas_call | solution.py:343

commit v2 on v1

--- a/solution.py
+++ b/solution.py
@@ -16,9 +16,10 @@
 PREV, NEXT, OWN, OPP = 0, 1, 2, 3
 QUARTER = 32
 COPIES = tuple(
-    ["ia", "ib", "ja", "jb", "fa", "fb", "t1a", "t1b", "t2", "t3a", "t3b", "u2"]
+    ["ia", "ib", "ja", "jb", "fa", "fb", "t1a", "t1b", "t2", "t3a", "t3b", "s3a", "s3b"]
     + ["w1", "w2", "w3", "ha", "hb", "sa", "sb", "dn0", "dn1", "dp0", "dp1"]
-    + [f"{name}{i}" for name in ("u3", "v1", "sw", "s", "q") for i in range(4)]
+    + [f"{name}{i}" for name in ("u3", "v1", "u2", "sw", "q") for i in range(4)]
+    + ["s0", "s1", "s2"]
 )
 
 
@@ -48,6 +49,8 @@
     prv = (lax.rem(n + NARROW - 2, NARROW), w)
     sib = (n + 1 - 2 * lax.rem(n, 2), w)
     hop = WIDE // 8
+    odd = lax.rem(w // hop, 2)
+    across = (n, w + hop - 2 * hop * odd)
     step1, back1 = (n, lax.rem(w + hop, WIDE)), (n, lax.rem(w + WIDE - hop, WIDE))
     step2, back2 = (n, lax.rem(w + 2 * hop, WIDE)), (n, lax.rem(w + WIDE - 2 * hop, WIDE))
 
@@ -73,18 +76,21 @@
         "t1b": (txt.at[0, 0, B], txt.at[1, 0, B], step1),
         "t3a": (txt.at[1, 0, A], txt.at[3, 0, A], step2),
         "t3b": (txt.at[1, 0, B], txt.at[3, 0, B], step2),
+        "s3a": (txt.at[3, 0, A], txt.at[3, 1, A], sib),
+        "s3b": (txt.at[3, 0, B], txt.at[3, 1, B], sib),
         "t2": (txt.at[0, 0], txt.at[2, 0], step2),
-        "u2": (txt_part.at[2, 0], got2, back2),
         "w1": (wts.at[0, 0], wts.at[1, 0], step1),
         "w2": (wts.at[0, 0], wts.at[2, 0], step2),
         "w3": (wts.at[1, 0], wts.at[3, 0], step2),
     }
     for i in range(4):
         plan[f"u3{i}"] = (txt_part.at[3, 0, part[i]], got3.at[part[i]], back2)
-        plan[f"v1{i}"] = (txt_part.at[1, 0, part[i]], got1.at[part[i]], back1)
+        plan[f"v1{i}"] = (txt_part.at[1, 0, part[i]], got1.at[part[i]], across)
+        plan[f"u2{i}"] = (txt_part.at[2, 0, part[i]], got2.at[part[i]], back2)
         plan[f"sw{i}"] = (wts.at[i, 0], wts.at[i, 1], sib)
+        plan[f"q{i}"] = (txt_part.at[i, 1], sib_part.at[i], sib)
+    for i in range(3):
         plan[f"s{i}"] = (txt.at[i, 0], txt.at[i, 1], sib)
-        plan[f"q{i}"] = (txt_part.at[i, 1], sib_part.at[i], sib)
     for i in range(2):
         low, high = part[i], part[2 + i]
         plan[f"dn{i}"] = (img_part.at[NEXT, high], from_prev.at[high], nxt)
@@ -168,13 +174,17 @@
         grads = factor / (1.0 + jnp.exp(-logits))
         g_h[rows, cols], g_l[rows, cols] = split(grads)
 
-    def image_grads(first, count):
-        rows = pl.ds(first * ROWS, count * ROWS)
+    def image_grads(first, count, begin=0, end=OFFSETS):
+        rows, inner = pl.ds(first * ROWS, count * ROWS), pl.ds(begin * PAIR, (end - begin) * PAIR)
         for tile in range(DIM // PAIR):
             cols = pl.ds(tile * PAIR, PAIR)
-            part = dot3((g_h[rows, :], g_l[rows, :]), (txt_h[:, cols], txt_l[:, cols]), 1, 0)
+            grads = dot3((g_h[rows, inner], g_l[rows, inner]), (txt_h[inner, cols], txt_l[inner, cols]), 1, 0)
             for slot in range(count):
-                img_part[first + slot, :, cols] = part[slot * ROWS:(slot + 1) * ROWS]
+                block = grads[slot * ROWS:(slot + 1) * ROWS]
+                if begin:
+                    img_part[first + slot, :, cols] += block
+                else:
+                    img_part[first + slot, :, cols] = block
 
     def text_grads(k):
         rows = pl.ds(k * PAIR, PAIR)
@@ -216,14 +226,18 @@
     pair_grads(PREV, 3, 1)
     arrived("w3")
     start("sw3")
-    arrived("t3a", "t3b")
-    start("s3")
+    image_grads(PREV, 3, 0, 3)
+    arrived("t3a")
+    start("s3a")
+    arrived("t3b")
+    start("s3b")
     split_text(3, 0)
-    arrived("s3", "sw3")
+    arrived("s3a", "s3b", "sw3")
     split_text(3, 1)
-    pair_grads(PREV, 3, 3)
-    image_grads(PREV, 2)
+    pair_grads(PREV, 2, 3)
+    image_grads(PREV, 2, 3, 4)
     start("dn0", "dp0")
+    pair_grads(OWN, 1, 3)
 
     arrived("fa", "fb")
     split_image(OPP)
@@ -257,11 +271,7 @@
             text_grads(0)
             start("q0")
         if i == 1:
-            image_grads(OWN, 1)
-    arrived("q2")
-    txt_part[2, 0] += sib_part[2]
-    sent("u33")
-    start("u2")
+            image_grads(OWN, 1, 3, 4)
     sent("ha", "hb")
     start("dn1", "dp1")
     arrived("ha")
@@ -270,13 +280,33 @@
     arrived("hb")
     img_part[PREV, B] += half_b[...]
     start("sb")
+    arrived("q2")
+    txt_part[2, 0] += sib_part[2]
+
+    @pl.when(odd == 0)
+    def _():
+        start("u20", "u21", "u22", "u23")
+
     arrived("q0")
     txt_part[0, 0] += sib_part[0]
 
+    @pl.when(odd == 1)
+    def _():
+        for i in range(4):
+            arrived(f"v1{i}")
+            txt_part[2, 0, part[i]] += got1[part[i]]
+            start(f"u2{i}")
+
     arrived("dn0", "dn1", "dp0", "dp1", "sa", "sb")
     img_sum[...] = img_part[OWN] + from_prev[...] + from_next[...]
-    arrived("u2", "v10", "v11", "v12", "v13")
-    txt_sum[...] = txt_part[0, 0] + got1[...] + got2[...]
+
+    @pl.when(odd == 0)
+    def _():
+        arrived("v10", "v11", "v12", "v13")
+        txt_part[0, 0] += got1[...]
+
+    arrived("u20", "u21", "u22", "u23")
+    txt_sum[...] = txt_part[0, 0] + got2[...]
     for name in COPIES:
         if name not in done:
             copy(name).wait_send()

time: 104 us -> 100 us (0.962)
  the two profiles are of different devices: /device:TPU:104 before, /device:TPU:120 now
where the time goes in v2:
time: 100 us
  Pallas kernels  98.1 us (98%)
  between operations  1.93 us (2%)
    pallas_call x1, Pallas kernels, on_device(): pl.pallas_call(kernel, out_shape=(out, out), in_specs=[anywhere] * 6, out...  95.3 us
    pallas_call x1, Pallas kernels, on_device(): pl.pallas_call(project_back, out_shape=(out, out), in_specs=[vmem] * 4, o...  2.75 us

profile of v2, /device:TPU:120, one launch (start us, length us, event | category | flops | bytes accessed | tf_op | source)
XLA Modules:
  0.0 100.0 jit_solution(3099168115224525881)
XLA Ops:
  1.9 95.3 %shard_map.77 = (f32[128,1024]{1,0:T(8,128)}, f32[128,1024]{1,0:T(8,128)}) custom-call(f32[128,1024]{1,0:T(8,128)} %img_ref.1, f32[128,1024]{1,0:T(8,128)} %txt_ref.1, s32[1,128]{1,0:T(1,128)} %bitcast.1, s32[109]{0:T(128)} %table_hbm.1, f32[1]{0:T(128)S(6)} %copy.8.scale_hbm, f32[1]{0:T(128)S(6)} %copy.9.bias_hbm), custom_call_target="tpu_custom_call" | custom-call | flops 9663676416 | bytes 2097152 | tf_op jit(solution)/shard_map/pallas_call | solution.py:332
  97.3 2.7 %shard_map.78 = (f32[128,1024]{1,0:T(8,128)}, f32[128,1024]{1,0:T(8,128)}) custom-call(f32[128,1024]{1,0:T(8,128)} %img_ref.1, f32[128,1024]{1,0:T(8,128)} %txt_ref.1, f32[128,1024]{1,0:T(8,128)} %get-tuple-element.4.img_sum, f32[128,1024]{1,0:T(8,128)} %get-tuple-element.5.txt_sum), custom_call_target="tpu_custom_call" | custom-call | flops 1048576 | bytes 3145728 | tf_op jit(solution)/shard_map/pallas_call | solution.py:373

commit v3 on v2

--- a/solution.py
+++ b/solution.py
@@ -39,7 +39,7 @@
 
 
 def kernel(
-    img_hbm, txt_hbm, ids_hbm, table_hbm, scale_hbm, bias_hbm, img_sum, txt_sum,
+    img_hbm, txt_hbm, ids_hbm, table_hbm, scale_hbm, bias_hbm, gimg_ref, gtxt_ref,
     raw, ids_ref, table_ref, scale_ref, bias_ref, load_sem, img, txt, wts, img_h, img_l, txt_h, txt_l, g_h, g_l, img_part, txt_part,
     half_a, half_b, from_prev, from_next, sib_part, got3, got1, got2, send_sem, recv_sem,
 ):
@@ -55,7 +55,7 @@
     step2, back2 = (n, lax.rem(w + 2 * hop, WIDE)), (n, lax.rem(w + WIDE - 2 * hop, WIDE))
 
     barrier = pltpu.get_barrier_semaphore()
-    partners = (nxt, prv, sib, step1, back1, step2, back2)
+    partners = (step1, back1, nxt, prv, step2, back2, sib)
     for partner in partners:
         pl.semaphore_signal(barrier, inc=1, device_id=partner, device_id_type=MESH)
 
@@ -297,8 +297,13 @@
             txt_part[2, 0, part[i]] += got1[part[i]]
             start(f"u2{i}")
 
+    def project_back(which, unit, hat_grad, out):
+        rows = raw[which]
+        inverse = lax.rsqrt(jnp.sum(rows * rows, axis=-1, keepdims=True) + 1e-06)
+        out[...] = inverse * (hat_grad - unit * jnp.sum(unit * hat_grad, axis=-1, keepdims=True))
+
     arrived("dn0", "dn1", "dp0", "dp1", "sa", "sb")
-    img_sum[...] = img_part[OWN] + from_prev[...] + from_next[...]
+    project_back(0, img[OWN], img_part[OWN] + from_prev[...] + from_next[...], gimg_ref)
 
     @pl.when(odd == 0)
     def _():
@@ -306,20 +311,15 @@
         txt_part[0, 0] += got1[...]
 
     arrived("u20", "u21", "u22", "u23")
-    txt_sum[...] = txt_part[0, 0] + got2[...]
+    project_back(1, txt[0, 0], txt_part[0, 0] + got2[...], gtxt_ref)
     for name in COPIES:
         if name not in done:
             copy(name).wait_send()
 
 
-def project_back(img_ref, txt_ref, img_sum, txt_sum, gimg_ref, gtxt_ref):
-    for rows, total, out in ((img_ref, img_sum, gimg_ref), (txt_ref, txt_sum, gtxt_ref)):
-        vectors = rows[...]
-        inverse = lax.rsqrt(jnp.sum(vectors * vectors, axis=-1, keepdims=True) + 1e-06)
-        unit = vectors * inverse
-        hat_grad = total[...]
-        along = jnp.sum(unit * hat_grad, axis=-1, keepdims=True)
-        out[...] = inverse * (hat_grad - unit * along)
+def copy_out(img_ref, txt_ref, gimg_ref, gtxt_ref):
+    gimg_ref[...] = img_ref[...]
+    gtxt_ref[...] = txt_ref[...]
 
 
 def on_device(images, texts, lang_ids, lang_table, log_scale, bias):
@@ -329,7 +329,7 @@
     block = (ROWS, DIM)
     half = (HALF, DIM)
     out = jax.ShapeDtypeStruct(block, f32)
-    img_sum, txt_sum = pl.pallas_call(
+    grads = pl.pallas_call(
         kernel,
         out_shape=(out, out),
         in_specs=[anywhere] * 6,
@@ -371,12 +371,12 @@
         ),
     )(images, texts, lang_ids.reshape(1, ROWS), lang_table, log_scale, bias)
     return pl.pallas_call(
-        project_back,
+        copy_out,
         out_shape=(out, out),
-        in_specs=[vmem] * 4,
+        in_specs=[vmem] * 2,
         out_specs=(vmem, vmem),
-        cost_estimate=pl.CostEstimate(flops=2**20, bytes_accessed=6 * 2**19, transcendentals=256),
-    )(images, texts, img_sum, txt_sum)
+        cost_estimate=pl.CostEstimate(flops=0, bytes_accessed=4 * 2**19, transcendentals=0),
+    )(*grads)
 
 
 def solution(mesh):

time: 100 us -> 99.8 us (level)
  no operation moved by 1% of the time
where the time goes in v3:
time: 99.8 us; the launch traced here: 99.6 us
  Pallas kernels  97.7 us (98%)
  between operations  1.93 us (2%)
    pallas_call x1, Pallas kernels, on_device(): pl.pallas_call(kernel, out_shape=(out, out), in_specs=[anywhere] * 6, out...  95.5 us
    pallas_call x1, Pallas kernels, on_device(): pl.pallas_call(copy_out, out_shape=(out, out), in_specs=[vmem] * 2, out_s...  2.2 us

profile of v3, /device:TPU:120, one launch (start us, length us, event | category | flops | bytes accessed | tf_op | source)
XLA Modules:
  0.0 99.6 jit_solution(4397576813897342221)
XLA Ops:
  1.9 95.5 %shard_map.77 = (f32[128,1024]{1,0:T(8,128)}, f32[128,1024]{1,0:T(8,128)}) custom-call(f32[128,1024]{1,0:T(8,128)} %img_hbm.1, f32[128,1024]{1,0:T(8,128)} %txt_hbm.1, s32[1,128]{1,0:T(1,128)} %bitcast.1, s32[109]{0:T(128)} %table_hbm.1, f32[1]{0:T(128)S(6)} %copy.8.scale_hbm, f32[1]{0:T(128)S(6)} %copy.9.bias_hbm), custom_call_target="tpu_custom_call" | custom-call | flops 9663676416 | bytes 2097152 | tf_op jit(solution)/shard_map/pallas_call | solution.py:332
  97.4 2.2 %shard_map.78 = (f32[128,1024]{1,0:T(8,128)}, f32[128,1024]{1,0:T(8,128)}) custom-call(f32[128,1024]{1,0:T(8,128)} %get-tuple-element.4.img_ref, f32[128,1024]{1,0:T(8,128)} %get-tuple-element.5.txt_ref), custom_call_target="tpu_custom_call" | custom-call | bytes 2097152 | tf_op jit(solution)/shard_map/pallas_call | solution.py:373

commit v4 on v3

--- a/solution.py
+++ b/solution.py
@@ -248,14 +248,14 @@
     pair_grads(OPP, 1, 0)
     arrived("q3")
     txt_part[3, 0] += sib_part[3]
-    start("u30")
+    start("u30", "u31")
     pair_grads(OPP, 1, 2)
     image_grads(OPP, 1)
     start("ha", "hb")
     text_grads(1)
     start("q1")
     sent("u30")
-    start("u31")
+    start("u32")
     text_grads(2)
     start("q2")
     arrived("q1")
@@ -264,9 +264,9 @@
         arrived(f"u3{i}")
         txt_part[1, 0, part[i]] += got3[part[i]]
         start(f"v1{i}")
-        if i < 2:
-            sent(f"u3{i + 1}")
-            start(f"u3{i + 2}")
+        if i == 0:
+            sent("u31")
+            start("u33")
         if i == 0:
             text_grads(0)
             start("q0")

time: 99.8 us -> 99.6 us (level)
  the two profiles are of different devices: /device:TPU:120 before, /device:TPU:126 now
where the time goes in v4:
time: 99.6 us; the launch traced here: 99.4 us
  Pallas kernels  97.5 us (98%)
  between operations  1.93 us (2%)
    pallas_call x1, Pallas kernels, on_device(): pl.pallas_call(kernel, out_shape=(out, out), in_specs=[anywhere] * 6, out...  95.3 us
    pallas_call x1, Pallas kernels, on_device(): pl.pallas_call(copy_out, out_shape=(out, out), in_specs=[vmem] * 2, out_s...  2.2 us

profile of v4, /device:TPU:126, one launch (start us, length us, event | category | flops | bytes accessed | tf_op | source)
XLA Modules:
  0.0 99.4 jit_solution(18170454044560273145)
XLA Ops:
  1.9 95.3 %shard_map.77 = (f32[128,1024]{1,0:T(8,128)}, f32[128,1024]{1,0:T(8,128)}) custom-call(f32[128,1024]{1,0:T(8,128)} %img_hbm.1, f32[128,1024]{1,0:T(8,128)} %txt_hbm.1, s32[1,128]{1,0:T(1,128)} %bitcast.1, s32[109]{0:T(128)} %table_hbm.1, f32[1]{0:T(128)S(6)} %copy.8.scale_hbm, f32[1]{0:T(128)S(6)} %copy.9.bias_hbm), custom_call_target="tpu_custom_call" | custom-call | flops 9663676416 | bytes 2097152 | tf_op jit(solution)/shard_map/pallas_call | solution.py:332
  97.2 2.2 %shard_map.78 = (f32[128,1024]{1,0:T(8,128)}, f32[128,1024]{1,0:T(8,128)}) custom-call(f32[128,1024]{1,0:T(8,128)} %get-tuple-element.4.img_ref, f32[128,1024]{1,0:T(8,128)} %get-tuple-element.5.txt_ref), custom_call_target="tpu_custom_call" | custom-call | bytes 2097152 | tf_op jit(solution)/shard_map/pallas_call | solution.py:373
